TPU v7x, 256 devices: a whole 4x4x8 slice. The times are simulated.
256 devices in a mesh: group: 8 (over x, core), leaf: 32 (over z, y).
Axes of the slice: x: 4, y: 4, z: 8, core: 2. Of those that a mesh axis runs over, the one named last changes fastest.
Arguments:
- panel_values: bfloat16 [64, 1048576], P(None, ('group', 'leaf')), may hold values from -6 to 6
- cluster_basis: bfloat16 [64, 1048576], P(None, ('group', 'leaf')), may hold values from -0.375 to 0.375
- near_blocks: bfloat16 [4096, 3, 256, 256], P(('group', 'leaf')), may hold values from -0.21875 to 0.21875
- near_list: int32 [4096, 3], P(('group', 'leaf')), may hold values from 0 to 4095, as said below
- transfer_leaf: bfloat16 [64, 262144], P(None, ('group', 'leaf')), may hold values from -0.375 to 0.375
- transfer_device: bfloat16 [64, 16384], replicated, may hold values from -0.5 to 0.5
- leaf_coupling: bfloat16 [64, 1572864], P(None, ('group', 'leaf')), may hold values from -0.3125 to 0.3125
- leaf_list: int32 [4096, 6], P(('group', 'leaf')), may hold values from 0 to 4095, as said below
- device_coupling: bfloat16 [64, 65536], P(None, ('group', 'leaf')), may hold values from -0.1875 to 0.1875
- device_list: int32 [256, 4], P(('group', 'leaf')), may hold values from 0 to 255, as said below
- group_coupling: bfloat16 [64, 1024], P(None, 'group'), may hold values from -0.125 to 0.125
- group_list: int32 [8, 2], P('group'), may hold values from 0 to 7, as said below
Outputs:
- product: bfloat16 [64, 1048576], P(None, ('group', 'leaf'))
Inputs may be any that keep to these rules, and one draw needn't show every extreme that they name: `near_list`: row t holds t itself first, then 3 - 1 distinct other leaves of the same group cluster, each at most 8 away from t. `leaf_list`: each row holds distinct leaves of the same group cluster as its leaf t, each more than 8 and at most 16 away from t. `device_list`: each row holds distinct device clusters of the same group cluster as its device cluster d, each 2 or more away from d. `group_list`: each row holds distinct group clusters other than its own.
All inputs are finite; a program needn't handle non-finite values.
Results may differ from a plain program's by a relative error of at most 0.0095.
Values may be sent and summed in bfloat16 or wider, within the bound.
A program may use at most 64 MiB of HBM per device.

v0:
```python
import jax
import jax.numpy as jnp
from jax import lax
from jax.sharding import PartitionSpec as P

NR = 8


def with_halo(cells, sides, width):
    for axis, dim in sides:
        count = lax.axis_size(axis)
        ends = count - 1
        head = lax.slice_in_dim(cells, 0, width, axis=dim)
        tail = lax.slice_in_dim(cells, cells.shape[dim] - width, cells.shape[dim], axis=dim)
        cells = jnp.concatenate(
            [
                lax.ppermute(tail, axis, [(i, (i + 1) % count) for i in range(ends)]),
                cells,
                lax.ppermute(head, axis, [((i + 1) % count, i) for i in range(ends)]),
            ],
            axis=dim,
        )
    return cells


def local(
    panel_values,
    cluster_basis,
    near_blocks,
    near_list,
    transfer_leaf,
    transfer_device,
    leaf_coupling,
    leaf_list,
    device_coupling,
    device_list,
    group_coupling,
    group_list,
):
    leaf_count = near_blocks.shape[0]
    leaf_size = near_blocks.shape[2]
    rank_size = cluster_basis.shape[0]
    rhs_count = panel_values.shape[0]
    leaf_links = leaf_list.shape[1]
    device_links = device_list.shape[1]
    group_links = group_list.shape[1]
    group_span = lax.axis_size("leaf")
    my_group = lax.axis_index("group")
    my_device = my_group * group_span + lax.axis_index("leaf")
    first_leaf = my_device * leaf_count
    panel_rows = panel_values.reshape(rhs_count, leaf_count, leaf_size)
    basis_rows = cluster_basis.reshape(rank_size, leaf_count, leaf_size)
    widened = with_halo(panel_values, (("leaf", 1),), NR * leaf_size)
    leaf_coefs = lax.dot_general(
        panel_rows, basis_rows, (((2,), (2,)), ((1,), (1,))), preferred_element_type=jnp.float32
    ).astype(jnp.bfloat16)
    flat_coefs = leaf_coefs.reshape(leaf_count, rhs_count * rank_size)
    coef_window = with_halo(flat_coefs, (("leaf", 0),), leaf_count)
    up_blocks = transfer_leaf.reshape(rank_size, leaf_count, rank_size)
    device_coefs = jnp.einsum(
        "lrb,alb->ra", leaf_coefs, up_blocks, preferred_element_type=jnp.float32
    ).astype(jnp.bfloat16)
    flat_device = device_coefs.reshape(1, rhs_count * rank_size)
    own_devices = lax.all_gather(flat_device, "leaf", axis=0, tiled=True)
    own_transfer = lax.dynamic_slice_in_dim(
        transfer_device, my_group * group_span * rank_size, group_span * rank_size, 1
    )
    own_group = jnp.einsum(
        "srb,asb->ra",
        own_devices.reshape(group_span, rhs_count, rank_size),
        own_transfer.reshape(rank_size, group_span, rank_size),
        preferred_element_type=jnp.float32,
    ).astype(jnp.bfloat16)
    group_coefs = lax.all_gather(
        own_group.reshape(1, rhs_count * rank_size), "group", axis=0, tiled=True
    )
    source_rows = jnp.take(coef_window, leaf_list - first_leaf + leaf_count, axis=0)
    source_rows = source_rows.reshape(leaf_count, leaf_links, rhs_count, rank_size)
    leaf_blocks = leaf_coupling.reshape(rank_size, leaf_count, leaf_links, rank_size)
    leaf_far = jnp.einsum(
        "tjrc,btjc->trb", source_rows, leaf_blocks, preferred_element_type=jnp.float32
    )
    near_rows = widened.reshape(rhs_count, leaf_count + 2 * NR, leaf_size)
    near_sources = jnp.take(near_rows, near_list - first_leaf + NR, axis=1)
    near_part = jnp.einsum(
        "rtjq,tjpq->rtp", near_sources, near_blocks, preferred_element_type=jnp.float32
    )
    group_sources = jnp.take(group_coefs, group_list[0], axis=0).reshape(
        group_links, rhs_count, rank_size
    )
    group_local = jnp.einsum(
        "jrc,bjc->rb",
        group_sources,
        group_coupling.reshape(rank_size, group_links, rank_size),
        preferred_element_type=jnp.float32,
    ).astype(jnp.bfloat16)
    device_sources = jnp.take(own_devices, device_list[0] - my_group * group_span, axis=0).reshape(
        device_links, rhs_count, rank_size
    )
    down_block = lax.dynamic_slice_in_dim(transfer_device, my_device * rank_size, rank_size, 1)
    device_local = jnp.einsum(
        "jrc,bjc->rb",
        device_sources,
        device_coupling.reshape(rank_size, device_links, rank_size),
        preferred_element_type=jnp.float32,
    )
    device_local = (
        device_local + jnp.dot(group_local, down_block, preferred_element_type=jnp.float32)
    ).astype(jnp.bfloat16)
    leaf_local = (
        leaf_far
        + jnp.einsum("ra,alb->lrb", device_local, up_blocks, preferred_element_type=jnp.float32)
    ).astype(jnp.bfloat16)
    far_part = jnp.einsum(
        "lrk,klp->rlp", leaf_local, basis_rows, preferred_element_type=jnp.float32
    )
    return (far_part + near_part).astype(jnp.bfloat16).reshape(rhs_count, leaf_count * leaf_size)


def solution(mesh):
    in_specs = (
        P(None, ("group", "leaf")),
        P(None, ("group", "leaf")),
        P(("group", "leaf"), None, None, None),
        P(("group", "leaf"), None),
        P(None, ("group", "leaf")),
        P(),
        P(None, ("group", "leaf")),
        P(("group", "leaf"), None),
        P(None, ("group", "leaf")),
        P(("group", "leaf"), None),
        P(None, "group"),
        P("group", None),
    )
    out_specs = P(None, ("group", "leaf"))
    return jax.shard_map(local, mesh=mesh, in_specs=in_specs, out_specs=out_specs, check_vma=False)
```

profile of v0, /device:TPU:1, one launch (start us, length us, event | category | flops | bytes accessed | tf_op | source)
XLA Modules:
  0.0 128.5 jit_solution(5951809749253580893)
XLA Ops:
  0.1 1.6 %convolution_convert_fusion = bf16[16,64,64]{2,1,0:T(8,128)(2,1)S(1)} fusion(bf16[8,16,8,256]{3,2,1,0:T(8,128)(2,1)} %bitcast.81, bf16[8,16,8,256]{3,2,1,0:T(8,128)(2,1)} %bitcast.84), kind=kOutput, calls=%fused_computation.20 | convolution fusion | flops 33619968 | bytes 1179648 | tf_op jit(solution)/shard_map/dot_general | solution.py:54
  2.0 1.3 %collective-permute-start.1 = (bf16[16,4096]{1,0:T(8,128)(2,1)S(1)}, bf16[16,4096]{1,0:T(8,128)(2,1)}, u32[]{:S(2)}, u32[]{:S(2)}) collective-permute-start(bf16[16,4096]{1,0:T(8,128)(2,1)S(1)} %reshape.128), channel_id=1, source_target_pairs={{1,0},{2,1},{3,2},{4,3},{5,4},{6,5},{7,6},{8,7},{9,8},{10,9},{11,1... | collective-permute-start | bytes 393224 | tf_op jit(solution)/shard_map/ppermute | solution.py:19
  3.3 5.3 %collective-permute-start = (bf16[16,4096]{1,0:T(8,128)(2,1)S(1)}, bf16[16,4096]{1,0:T(8,128)(2,1)}, u32[]{:S(2)}, u32[]{:S(2)}) collective-permute-start(bf16[16,4096]{1,0:T(8,128)(2,1)S(1)} %reshape.128), channel_id=1, source_target_pairs={{0,1},{1,2},{2,3},{3,4},{4,5},{5,6},{6,7},{7,8},{8,9},{9,10},{10,1... | collective-permute-start | bytes 393224 | tf_op jit(solution)/shard_map/ppermute | solution.py:17
  8.6 0.8 fusion.70
  9.4 3.4 %collective-permute-start.2 = (bf16[64,2048]{1,0:T(8,128)(2,1)}, bf16[64,2048]{1,0:T(8,128)(2,1)}, u32[]{:S(2)}, u32[]{:S(2)}) collective-permute-start(bf16[64,2048]{1,0:T(8,128)(2,1)} %get-tuple-element.9), channel_id=1, source_target_pairs={{0,1},{1,2},{2,3},{3,4},{4,5},{5,6},{6,7},{7,8},{8,9},{9,10},{10,1... | collective-permute-start | bytes 786440 | tf_op jit(solution)/shard_map/ppermute | solution.py:17
  12.9 1.3 collective-permute-start.3
  16.5 0.6 compare_and_fusion.1
  18.3 0.7 reshape.136
  19.0 0.7 reshape.132
  20.8 44.4 %all-gather = bf16[32,1,4096]{2,1,0:T(2,128)(2,1)S(1)} all-gather(bf16[1,1,4096]{2,1,0:T(2,128)(2,1)S(1)} %reshape.176), channel_id=1, replica_groups=mesh['group'=8,'leaf'=32] {'leaf'}, dimensions={0}, use_global_device_ids=true | all-gather | bytes 270336 | tf_op jit(solution)/shard_map/all_gather | solution.py:64
  65.2 1.0 copy.128
  66.2 2.2 %reduce = bf16[32,4096]{1,0:T(8,128)(2,1)} reduce(bf16[32,1,4096]{2,1,0:T(2,128)(2,1)S(1)} %all-gather, bf16[]{:T(256)} %constant.84), dimensions={1}, to_apply=%all-gather.reduce_sub_computation | reduce | bytes 524290 | tf_op jit(solution)/shard_map/all_gather | solution.py:64
  68.5 1.7 %gather_fusion.1 = bf16[4,4096]{1,0:T(4,128)(2,1)S(1)} fusion(bf16[32,4096]{1,0:T(8,128)(2,1)} %bitcast.82, s32[1024]{0:T(1024)} %pad_clamp_fusion.2), kind=kCustom, calls=%fused_computation.1 | custom fusion | bytes 65552 | tf_op jit(solution)/shard_map/jit(_take)/gather | solution.py:97
  70.2 0.8 gather.25
  70.9 1.5 %reshape.133 = bf16[32,64,64]{2,1,0:T(8,128)(2,1)S(1)} reshape(bf16[32,4096]{1,0:T(8,128)(2,1)} %reduce) | data formatting | bytes 524288 | tf_op jit(solution)/shard_map/reshape | solution.py:70
  72.8 26.1 %all-gather.1 = bf16[8,1,4096]{2,1,0:T(2,128)(2,1)S(1)} all-gather(bf16[1,1,4096]{2,1,0:T(2,128)(2,1)S(1)} %reshape.178), channel_id=1, replica_groups=mesh['group'=8,'leaf'=32] {'group'}, dimensions={0}, use_global_device_ids=true | all-gather | bytes 73728 | tf_op jit(solution)/shard_map/all_gather | solution.py:74
  99.0 0.7 gather_fusion.2
  99.8 1.1 convolution_bitcast_fusion.3
  100.9 1.1 fusion.32
  102.0 1.0 convolution_bitcast_fusion
  103.6 0.8 copy.79
  104.4 0.8 copy.68
  105.1 0.7 copy.80
  106.0 2.9 %reshape.129 = bf16[64,16,6,64]{3,2,1,0:T(8,128)(2,1)} reshape(bf16[64,6144]{1,0:T(8,128)(2,1)S(1)} %copy-done.3) | data formatting | bytes 1572864 | tf_op jit(solution)/shard_map/reshape | solution.py:79
  108.9 1.0 pad_maximum_fusion.1
  109.9 1.0 gather_fusion
  110.9 2.6 %gather.23 = bf16[16,6,64,64]{3,2,1,0:T(8,128)(2,1)} reshape(bf16[96,4096]{1,0:T(8,128)(2,1)S(1)} %gather_fusion) | data formatting | bytes 1572864 | tf_op jit(solution)/shard_map/jit(_take)/gather | solution.py:77
  113.5 1.1 pad_maximum_fusion
  114.8 1.9 %gather_fusion.3 = bf16[48,64,256]{2,1,0:T(8,128)(2,1)} fusion(bf16[64,32,256]{2,0,1:T(8,128)(2,1)S(1)} %bitcast.78, s32[1024]{0:T(1024)S(1)} %pad_clamp_fusion), kind=kCustom, calls=%fused_computation.3 | custom fusion | bytes 3145920 | tf_op jit(solution)/shard_map/jit(_take)/gather | solution.py:84
  116.6 5.3 %fusion.8 = f32[16,64,256]{2,1,0:T(8,128)S(1)} fusion(bf16[16,3,256,256]{3,2,1,0:T(8,128)(2,1)} %param.14, bf16[16,3,64,256]{3,2,1,0:T(8,128)(2,1)} %bitcast.79, pred[16,3]{1,0:T(8,128)(4,1)S(1)} %copy.79), kind=kOutput, calls=%fused_computation.12 | convolution fusion | flops 403439616 | bytes 8912944 | tf_op jit(solution)/shard_map/rtjq,tjpq->rtp/dot_general | solution.py:85
  121.9 4.7 %fusion.12 = bf16[16,8,8,256]{3,2,1,0:T(8,128)(2,1)} fusion(f32[16,64,256]{2,1,0:T(8,128)S(1)} %fusion.8, f32[16,64,64]{2,1,0:T(8,128)} %convolution_bitcast_fusion, bf16[64,16,6,64]{3,2,1,0:T(8,128)(2,1)} %reshape.129, bf16[16,6,64,64]{3,2,1,0:T(8,128)(2,1)} %gather.23, pred[16,6]{1,0:T(8,128)(4,1)S(1)} %copy.68, bf16[8,16,8,256]{3,2,1,0:T(8,128)(2,1)} %bitcast.85), kind=kOutput, calls=%fused_computation.15 | convolution fusion | flops 84934656 | bytes 3932256 | tf_op jit(solution)/shard_map/lrk,klp->rlp/dot_general | solution.py:114
  126.6 1.9 %copy.90 = bf16[16,8,8,256]{3,2,0,1:T(8,128)(2,1)} copy(bf16[16,8,8,256]{3,2,1,0:T(8,128)(2,1)} %fusion.12) | data formatting | bytes 1048576 | tf_op jit(solution)/shard_map/reshape | solution.py:117
  (49 shorter events, 6.3 us)
Async XLA Ops:
  0.0 20.2 %copy-start = (bf16[64,16384]{1,0:T(8,128)(2,1)S(1)}, bf16[64,16384]{1,0:T(8,128)(2,1)}, u32[]{:S(2)}) copy-start(bf16[64,16384]{1,0:T(8,128)(2,1)} %param.17) | copy-start | bytes 6291460
  0.0 8.6 %copy-start.1 = (bf16[64,4096]{1,0:T(8,128)(2,1)S(1)}, bf16[64,4096]{1,0:T(8,128)(2,1)}, u32[]{:S(2)}) copy-start(bf16[64,4096]{1,0:T(8,128)(2,1)} %param.12) | copy-start | bytes 1572868
  0.0 14.2 %copy-start.9 = (s32[1,4]{1,0:T(1,128)S(1)}, s32[1,4]{1,0:T(1,128)}, u32[]{:S(2)}) copy-start(s32[1,4]{1,0:T(1,128)} %param.21) | copy-start | bytes 52
  0.0 14.7 %copy-start.10 = (s32[1,2]{1,0:T(1,128)S(1)}, s32[1,2]{1,0:T(1,128)}, u32[]{:S(2)}) copy-start(s32[1,2]{1,0:T(1,128)} %param.23) | copy-start | bytes 28
  0.0 16.4 %copy-start.8 = (s32[16,3]{0,1:T(4,128)S(1)}, s32[16,3]{0,1:T(4,128)}, u32[]{:S(2)}) copy-start(s32[16,3]{0,1:T(4,128)} %param.15) | copy-start | bytes 580
  0.0 17.0 %copy-start.7 = (s32[16,6]{0,1:T(8,128)S(1)}, s32[16,6]{0,1:T(8,128)}, u32[]{:S(2)}) copy-start(s32[16,6]{0,1:T(8,128)} %param.19) | copy-start | bytes 1156
  0.0 18.3 %copy-start.6 = (bf16[64,128]{1,0:T(8,128)(2,1)S(1)}, bf16[64,128]{1,0:T(8,128)(2,1)}, u32[]{:S(2)}) copy-start(bf16[64,128]{1,0:T(8,128)(2,1)} %param.22) | copy-start | bytes 49156
  0.1 19.0 %copy-start.5 = (bf16[64,256]{1,0:T(8,128)(2,1)S(1)}, bf16[64,256]{1,0:T(8,128)(2,1)}, u32[]{:S(2)}) copy-start(bf16[64,256]{1,0:T(8,128)(2,1)} %param.20) | copy-start | bytes 98308
  0.1 19.7 %copy-start.4 = (bf16[64,1024]{1,0:T(8,128)(2,1)S(1)}, bf16[64,1024]{1,0:T(8,128)(2,1)}, u32[]{:S(2)}) copy-start(bf16[64,1024]{1,0:T(8,128)(2,1)} %param.16) | copy-start | bytes 393220
  2.0 106.9 %collective-permute-start.1 = (bf16[16,4096]{1,0:T(8,128)(2,1)S(1)}, bf16[16,4096]{1,0:T(8,128)(2,1)}, u32[]{:S(2)}, u32[]{:S(2)}) collective-permute-start(bf16[16,4096]{1,0:T(8,128)(2,1)S(1)} %reshape.128), channel_id=1, source_target_pairs={{1,0},{2,1},{3,2},{4,3},{5,4},{6,5},{7,6},{8,7},{9,8},{10,9},{11,1... | collective-permute-start | bytes 393224 | tf_op jit(solution)/shard_map/ppermute | solution.py:19
  3.3 105.6 %collective-permute-start = (bf16[16,4096]{1,0:T(8,128)(2,1)S(1)}, bf16[16,4096]{1,0:T(8,128)(2,1)}, u32[]{:S(2)}, u32[]{:S(2)}) collective-permute-start(bf16[16,4096]{1,0:T(8,128)(2,1)S(1)} %reshape.128), channel_id=1, source_target_pairs={{0,1},{1,2},{2,3},{3,4},{4,5},{5,6},{6,7},{7,8},{8,9},{9,10},{10,1... | collective-permute-start | bytes 393224 | tf_op jit(solution)/shard_map/ppermute | solution.py:17
  9.4 104.1 %collective-permute-start.2 = (bf16[64,2048]{1,0:T(8,128)(2,1)}, bf16[64,2048]{1,0:T(8,128)(2,1)}, u32[]{:S(2)}, u32[]{:S(2)}) collective-permute-start(bf16[64,2048]{1,0:T(8,128)(2,1)} %get-tuple-element.9), channel_id=1, source_target_pairs={{0,1},{1,2},{2,3},{3,4},{4,5},{5,6},{6,7},{7,8},{8,9},{9,10},{10,1... | collective-permute-start | bytes 786440 | tf_op jit(solution)/shard_map/ppermute | solution.py:17
  12.9 100.7 %collective-permute-start.3 = (bf16[64,2048]{1,0:T(8,128)(2,1)}, bf16[64,2048]{1,0:T(8,128)(2,1)}, u32[]{:S(2)}, u32[]{:S(2)}) collective-permute-start(bf16[64,2048]{1,0:T(8,128)(2,1)} %get-tuple-element.10), channel_id=1, source_target_pairs={{1,0},{2,1},{3,2},{4,3},{5,4},{6,5},{7,6},{8,7},{9,8},{10,9},{11,1... | collective-permute-start | bytes 786440 | tf_op jit(solution)/shard_map/ppermute | solution.py:19
  72.7 33.2 %copy-start.3 = (bf16[64,6144]{1,0:T(8,128)(2,1)S(1)}, bf16[64,6144]{1,0:T(8,128)(2,1)}, u32[]{:S(2)}) copy-start(bf16[64,6144]{1,0:T(8,128)(2,1)} %param.18) | copy-start | bytes 2359300
  110.9 2.6 %copy-start.2 = (bf16[64,4096]{1,0:T(8,128)(2,1)S(1)}, bf16[64,4096]{1,0:T(8,128)(2,1)}, u32[]{:S(2)}) copy-start(bf16[64,4096]{1,0:T(8,128)(2,1)} %param.12) | copy-start | bytes 1572868
where the time goes:
time: 129 us; the launch traced here: 128 us
  blocking collectives  70.5 us (55%)
  local copies, waits for them, and re-layouts  22.7 us (18%)
  matrix products  15.3 us (12%)
  starting transfers between devices  11.3 us (9%)
  other arithmetic  8.4 us (7%)
    all_gather x1, blocking collectives, local(): own_devices = lax.all_gather(flat_device, 'leaf', axis=0, tiled=True)  44.4 us
    all_gather x1, blocking collectives, local(): lax.all_gather(own_group.reshape(1, rhs_count * rank_size), 'group', axis...  26.1 us
    ppermute x2, starting transfers between devices, with_halo(): lax.ppermute(tail, axis, [(i, (i + 1) % count) for i in range(ends)])  8.74 us
    dot_general x1, matrix products, local(): jnp.einsum('rtjq,tjpq->rtp', near_sources, near_blocks, preferred_element...  5.29 us
    dot_general x1, matrix products, local(): jnp.einsum('lrk,klp->rlp', leaf_local, basis_rows, preferred_element_type...  4.69 us
    gather x2, local copies, waits for them, and re-layouts, local(): jnp.take(coef_window, leaf_list - first_leaf + leaf_count, axis=0)  3.63 us
    reshape x1, local copies, waits for them, and re-layouts, local(): leaf_coupling.reshape(rank_size, leaf_count, leaf_links, rank_size)  2.89 us
  transfers between devices with their start and end apart: 4, of which 0 were waited for; matrix products, arithmetic and copies ran while one was open for 23% of the time, Pallas kernels for 0%

commit v1 on v0

v1 whole, which is shorter than its diff:
```python
import functools

import jax
import jax.numpy as jnp
from jax import lax
from jax.experimental import pallas as pl
from jax.experimental.pallas import tpu as pltpu
from jax.sharding import PartitionSpec as P

ROW = 4
MESH = pl.DeviceIdType.MESH
F32 = jnp.float32
BF16 = jnp.bfloat16


def nt(a, b):
    return lax.dot_general(a, b, (((1,), (1,)), ((), ())), preferred_element_type=F32)


def nn(a, b):
    return jnp.dot(a, b, preferred_element_type=F32)


def low_lanes(shape):
    return lax.broadcasted_iota(jnp.int32, shape, 1) % 128 < 64


def fold_rows(wide):
    half = wide.shape[0] // 2
    return jnp.where(low_lanes((half, 128)), wide[:half], wide[half:])


def unfold_rows(packed):
    low = low_lanes(packed.shape)
    zero = jnp.zeros_like(packed)
    return jnp.concatenate([jnp.where(low, packed, zero), jnp.where(low, zero, packed)], axis=0)


def spreader():
    row = lax.broadcasted_iota(jnp.int32, (128, 256), 0)
    col = lax.broadcasted_iota(jnp.int32, (128, 256), 1)
    return jnp.where(row == col // 128 * 64 + col % 64, 1.0, 0.0).astype(BF16)


def spread(x):
    pieces = [x[:, i : i + 128] for i in range(0, x.shape[1], 128)]
    wide = [nn(piece, spreader()).astype(BF16) for piece in pieces]
    return jnp.concatenate(wide, axis=1)


def clamp(index, count):
    return jnp.minimum(jnp.maximum(index, 0), count - 1)


def kernel(
    groups, span, leaves, rank, ls, leaf_links, device_links, group_links, reach,
    panel, basis, near, near_list, transfer_leaf, transfer_device, leaf_coupling, leaf_list,
    device_coupling, device_list, group_coupling, group_list,
    out,
    p_own, b_own, nb_self, nb_rest, t_own, td_group, lc, dc, gc,
    halo_a, halo_b, c_own, halo_c, dbuf, pgbuf, gbuf,
    w, acc, lf, td_dup,
    load_sem, halo_send, halo_recv, row_send, row_recv, col_send, col_recv, drow_send, drow_recv,
    grp_send, grp_recv,
):
    gi = lax.axis_index("group")
    li = lax.axis_index("leaf")
    zi = li // ROW
    yi = li % ROW
    cols = span // ROW
    first_leaf = (gi * span + li) * leaves
    half = reach // 2
    left = zi * ROW + lax.rem(yi + ROW - 1, ROW)
    right = zi * ROW + lax.rem(yi + 1, ROW)
    at_start, at_end = yi == 0, yi == ROW - 1
    next_z = jnp.where(at_start, lax.rem(zi + 1, cols), lax.rem(zi + cols - 1, cols)) * ROW + yi

    row_peers = [zi * ROW + lax.rem(yi + k, ROW) for k in range(1, ROW)]
    col_peers = [lax.rem(zi + k, cols) * ROW + yi for k in range(1, cols)]
    grp_peers = [lax.rem(gi + k, groups) for k in range(1, groups)]

    barrier = pltpu.get_barrier_semaphore()
    for peer in row_peers + col_peers:
        pl.semaphore_signal(barrier, inc=1, device_id=(gi, peer), device_id_type=MESH)
    for peer in grp_peers:
        pl.semaphore_signal(barrier, inc=1, device_id=(peer, li), device_id_type=MESH)

    def load(i, src, dst):
        copy = pltpu.make_async_copy(src, dst, load_sem.at[i])
        copy.start()
        return copy

    for leaf in range(leaves):
        pltpu.make_async_copy(panel.at[:, pl.ds(leaf * ls, ls)], p_own.at[leaf], load_sem.at[0]).start()
    load_p = pltpu.make_async_copy(p_own, p_own, load_sem.at[0])
    load_b = load(1, basis, b_own)
    load_t = load(2, transfer_leaf, t_own)
    group_start = pl.multiple_of(gi * span * rank, span * rank)
    load_td = load(3, transfer_device.at[:, pl.ds(group_start, span * rank)], td_group)
    load_self = load(4, near.at[:, 0], nb_self)
    load_lc = load(5, leaf_coupling, lc)
    load_gc = load(6, group_coupling, gc)
    load_dc = load(7, device_coupling, dc)
    load_rest = load(8, near.at[:, pl.ds(1, 2)], nb_rest)

    def send(src, dst, send_sem, recv_sem, device):
        copy = pltpu.make_async_remote_copy(
            src_ref=src, dst_ref=dst, send_sem=send_sem, recv_sem=recv_sem,
            device_id=device, device_id_type=MESH,
        )
        copy.start()
        return copy

    low = low_lanes((64, 128))
    load_p.wait()
    load_b.wait()
    for pair in range(leaves // 2):
        wide = []
        for leaf in (2 * pair, 2 * pair + 1):
            basis_leaf = b_own[:, leaf * ls : (leaf + 1) * ls]
            twice = jnp.concatenate([basis_leaf, basis_leaf], axis=0)
            coefs = nt(p_own[leaf], twice)
            w[leaves + leaf] = coefs.astype(BF16)
            wide.append(coefs)
        c_own[:, pair * 128 : (pair + 1) * 128] = jnp.where(low, wide[0], wide[1]).astype(BF16)

    load_t.wait()
    transfer = t_own[...]
    own_d = nt(c_own[...], jnp.concatenate([transfer, transfer], axis=0))
    own_slot = yi * cols + zi
    dbuf[own_slot] = fold_rows(own_d).astype(BF16)

    pl.semaphore_wait(barrier, (ROW - 1) + (cols - 1) + (groups - 1))

    col_copies = [
        send(dbuf.at[own_slot], dbuf.at[own_slot], col_send.at[k], col_recv.at[k], (gi, peer))
        for k, peer in enumerate(col_peers)
    ]
    to_right, to_left = jnp.where(at_end, 2, 0), jnp.where(at_start, 2, 1)
    edges = {
        "c": (halo_c, 0, c_own, c_own),
        "a": (halo_a, 3, p_own.at[pl.ds(leaves - half, half)], p_own.at[pl.ds(0, half)]),
        "b": (halo_b, 6, p_own.at[pl.ds(leaves - 2 * half, half)], p_own.at[pl.ds(half, half)]),
    }
    halo_copies = []

    def halo_copy(name, src, slot, k, device):
        buffer, base = edges[name][:2]
        return pltpu.make_async_remote_copy(
            src_ref=src, dst_ref=buffer.at[slot], send_sem=halo_send.at[base + k],
            recv_sem=halo_recv.at[base + slot], device_id=(gi, device), device_id_type=MESH,
        )

    def send_halo(name):
        for k, (slot, device) in enumerate(((to_right, right), (to_left, left))):
            copy = halo_copy(name, edges[name][2 + k], slot, k, device)
            copy.start()
            halo_copies.append(copy)

    def hand_on(name):
        @pl.when(at_start | at_end)
        def _():
            buffer = edges[name][0]
            halo_copy(name, buffer.at[2], 2, 2, next_z).wait_recv()
            halo_copy(name, buffer.at[2], jnp.where(at_start, 0, 1), 2, next_z).start()

    def wait_halo(name):
        for slot in (0, 1):
            halo_copy(name, edges[name][0].at[2], slot, 2, next_z).wait_recv()

    def end_halo(name):
        @pl.when(at_start | at_end)
        def _():
            halo_copy(name, edges[name][0].at[2], 0, 2, next_z).wait_send()

    send_halo("c")
    send_halo("a")

    load_td.wait()
    for j in range(cols):
        tile = pl.multiple_of((j * ROW + yi - yi % 2) * rank, 128)
        td_dup[:, j * 256 : (j + 1) * 256] = spread(td_group[:, pl.ds(tile, 128)])

    def td_of(j):
        return td_dup[:, pl.ds(pl.multiple_of(j * 256 + yi % 2 * 128, 128), 128)]

    def near_self(first, last):
        for leaf in range(first, last):
            lanes = slice(leaf * ls, (leaf + 1) * ls)
            acc[:, lanes] = nt(p_own[leaf], nb_self[leaf])

    load_self.wait()
    near_self(0, leaves)
    load_gc.wait()
    gc_dup = spread(gc[...])
    load_dc.wait()
    dc_dup = spread(dc[...])
    td_wide = jnp.concatenate([td_of(j) for j in range(cols)], axis=1)
    td_wide = jnp.concatenate([td_wide, td_wide], axis=0)

    for copy in col_copies:
        copy.wait()
    col_d = jnp.concatenate([dbuf[yi * cols + j] for j in range(cols)], axis=1)
    pgbuf[yi] = fold_rows(nt(unfold_rows(col_d), td_wide))
    pg_copies = [
        send(pgbuf.at[yi], pgbuf.at[yi], row_send.at[k], row_recv.at[k], (gi, peer))
        for k, peer in enumerate(row_peers)
    ]
    send_halo("b")
    mine = pl.ds(yi * cols, cols)
    d_copies = [
        send(dbuf.at[mine], dbuf.at[mine], drow_send.at[k], drow_recv.at[k], (gi, peer))
        for k, peer in enumerate(row_peers)
    ]

    hand_on("c")
    hand_on("a")

    for copy in pg_copies:
        copy.wait()
    total = pgbuf[0]
    for j in range(1, ROW):
        total = total + pgbuf[j]
    gbuf[gi] = total.astype(BF16)
    g_copies = [
        send(gbuf.at[gi], gbuf.at[gi], grp_send.at[k], grp_recv.at[k], (peer, li))
        for k, peer in enumerate(grp_peers)
    ]

    hand_on("b")

    load_lc.wait()
    wait_halo("c")
    for slot, start in ((0, 0), (1, 2 * leaves)):
        for pair in range(leaves // 2):
            wide = nn(halo_c[slot, :, pair * 128 : (pair + 1) * 128], spreader()).astype(BF16)
            w[start + 2 * pair] = wide[:, :128]
            w[start + 2 * pair + 1] = wide[:, 128:]

    for pair in range(leaves // 2):
        sources = []
        matrices = []
        for leaf in (2 * pair, 2 * pair + 1):
            found = [w[clamp(leaf_list[j, leaf] - first_leaf + leaves, 3 * leaves)] for j in range(leaf_links)]
            halves = [jnp.where(low, found[j], found[j + 1]) for j in range(0, leaf_links, 2)]
            sources.append(jnp.concatenate(halves, axis=1))
            matrices.append(lc[:, leaf * leaf_links * rank : (leaf + 1) * leaf_links * rank])
        far = nt(jnp.concatenate(sources, axis=0), jnp.concatenate(matrices, axis=0))
        lf[:, pair * 128 : (pair + 1) * 128] = jnp.where(low, far[:64], far[64:])

    def leaf_of(buffer, index, count):
        return buffer[clamp(index, count)]

    def near_source(leaf, source):
        own = leaf_of(p_own, source, leaves)
        if leaf < reach:
            found = jnp.where(source >= 0, own, leaf_of(halo_a.at[0], source + half, half))
            if leaf < half:
                found = jnp.where(source < -half, leaf_of(halo_b.at[0], source + 2 * half, half), found)
        else:
            past = source - leaves
            found = jnp.where(past < 0, own, leaf_of(halo_a.at[1], past, half))
            if leaf >= leaves - half:
                found = jnp.where(past >= half, leaf_of(halo_b.at[1], past - half, half), found)
        return found

    def near_rest(leaf):
        found = [near_source(leaf, near_list[j, leaf] - first_leaf) for j in (1, 2)]
        blocks = [nb_rest[leaf, 0], nb_rest[leaf, 1]]
        return nt(jnp.concatenate(found, axis=1), jnp.concatenate(blocks, axis=1))

    load_rest.wait()
    wait_halo("a")
    for leaf in range(half, leaves - half):
        acc[:, leaf * ls : (leaf + 1) * ls] += near_rest(leaf)

    for copy in d_copies:
        copy.wait()
    places = [clamp(device_list[0, j] - gi * span, span) for j in range(device_links)]
    found = [dbuf[place % ROW * cols + place // ROW] for place in places]
    d_far = nt(unfold_rows(jnp.concatenate(found, axis=1)), dc_dup)
    for copy in g_copies:
        copy.wait()
    found = [gbuf[clamp(group_list[0, j], groups)] for j in range(group_links)]
    g_local = nt(unfold_rows(jnp.concatenate(found, axis=1)), gc_dup).astype(BF16)
    td_own = td_of(zi)[:, :rank]
    d_local = (d_far + nn(g_local, td_own)).astype(BF16)
    l_local = (lf[...] + nn(d_local, t_own[...])).astype(BF16)
    for pair in range(leaves // 2):
        x = l_local[:, pair * 128 : (pair + 1) * 128]
        zero = jnp.zeros_like(x)
        stacked = jnp.concatenate([jnp.where(low, x, zero), jnp.where(low, zero, x)], axis=0)
        first = slice(2 * pair * ls, (2 * pair + 1) * ls)
        second = slice((2 * pair + 1) * ls, (2 * pair + 2) * ls)
        far = nn(stacked, jnp.concatenate([b_own[:, first], b_own[:, second]], axis=0))
        for leaf, lanes, part in ((2 * pair, first, far[:64]), (2 * pair + 1, second, far[64:])):
            if half <= leaf < leaves - half:
                out[:, lanes] = (acc[:, lanes] + part).astype(BF16)
            else:
                acc[:, lanes] = acc[:, lanes] + part

    wait_halo("b")
    for leaf in list(range(half)) + list(range(leaves - half, leaves)):
        lanes = slice(leaf * ls, (leaf + 1) * ls)
        out[:, lanes] = (acc[:, lanes] + near_rest(leaf)).astype(BF16)

    for copy in halo_copies:
        copy.wait_send()
    for name in edges:
        end_halo(name)


def local(
    panel_values,
    cluster_basis,
    near_blocks,
    near_list,
    transfer_leaf,
    transfer_device,
    leaf_coupling,
    leaf_list,
    device_coupling,
    device_list,
    group_coupling,
    group_list,
):
    rhs, width = panel_values.shape
    leaves, near_links, ls, _ = near_blocks.shape
    rank = cluster_basis.shape[0]
    groups = lax.axis_size("group")
    span = lax.axis_size("leaf")
    cols = span // ROW
    reach = leaves // 2
    half = reach // 2
    leaf_links = leaf_list.shape[1]
    device_links = device_list.shape[1]
    group_links = group_list.shape[1]
    coefs = leaves * rank
    hbm = pl.BlockSpec(memory_space=pltpu.HBM)
    smem = pl.BlockSpec(memory_space=pltpu.SMEM)
    sizes = (groups, span, leaves, rank, ls, leaf_links, device_links, group_links, reach)
    dma = pltpu.SemaphoreType.DMA
    halo = pltpu.VMEM((3, half, rhs, ls), BF16)
    return pl.pallas_call(
        functools.partial(kernel, *sizes),
        out_shape=jax.ShapeDtypeStruct((rhs, width), BF16),
        in_specs=[hbm, hbm, hbm, smem, hbm, hbm, hbm, smem, hbm, smem, hbm, smem],
        out_specs=pl.BlockSpec(memory_space=pltpu.VMEM),
        scratch_shapes=[
            pltpu.VMEM((leaves, rhs, ls), BF16),
            pltpu.VMEM((rank, width), BF16),
            pltpu.VMEM((leaves, ls, ls), BF16),
            pltpu.VMEM((leaves, near_links - 1, ls, ls), BF16),
            pltpu.VMEM((rank, coefs), BF16),
            pltpu.VMEM((rank, span * rank), BF16),
            pltpu.VMEM((rank, leaf_links * coefs), BF16),
            pltpu.VMEM((rank, device_links * rank), BF16),
            pltpu.VMEM((rank, group_links * rank), BF16),
            halo,
            halo,
            pltpu.VMEM((rhs, coefs), BF16),
            pltpu.VMEM((3, rhs, coefs), BF16),
            pltpu.VMEM((span, rhs // 2, 2 * rank), BF16),
            pltpu.VMEM((ROW, rhs // 2, 2 * rank), F32),
            pltpu.VMEM((groups, rhs // 2, 2 * rank), BF16),
            pltpu.VMEM((3 * leaves, rhs, 2 * rank), BF16),
            pltpu.VMEM((rhs, width), F32),
            pltpu.VMEM((rhs, coefs), F32),
            pltpu.VMEM((rank, cols * 4 * rank), BF16),
            dma((9,)),
            dma((9,)),
            dma((9,)),
            dma((ROW - 1,)),
            dma((ROW - 1,)),
            dma((cols - 1,)),
            dma((cols - 1,)),
            dma((ROW - 1,)),
            dma((ROW - 1,)),
            dma((groups - 1,)),
            dma((groups - 1,)),
        ],
        compiler_params=pltpu.CompilerParams(
            collective_id=0, has_side_effects=True, vmem_limit_bytes=60 * 1024 * 1024
        ),
        cost_estimate=pl.CostEstimate(flops=500_000_000, bytes_accessed=10_000_000, transcendentals=0),
    )(
        panel_values,
        cluster_basis,
        near_blocks,
        near_list.T,
        transfer_leaf,
        transfer_device,
        leaf_coupling,
        leaf_list.T,
        device_coupling,
        device_list,
        group_coupling,
        group_list,
    )


def solution(mesh):
    in_specs = (
        P(None, ("group", "leaf")),
        P(None, ("group", "leaf")),
        P(("group", "leaf"), None, None, None),
        P(("group", "leaf"), None),
        P(None, ("group", "leaf")),
        P(),
        P(None, ("group", "leaf")),
        P(("group", "leaf"), None),
        P(None, ("group", "leaf")),
        P(("group", "leaf"), None),
        P(None, "group"),
        P("group", None),
    )
    out_specs = P(None, ("group", "leaf"))
    return jax.shard_map(local, mesh=mesh, in_specs=in_specs, out_specs=out_specs, check_vma=False)
```

time: 129 us -> 30.5 us (0.24)
  blocking collectives: 70.5 us -> 0 us
  Pallas kernels: 0 us -> 28.4 us
  local copies, waits for them, and re-layouts: 22.7 us -> 1.87 us
  matrix products: 15.3 us -> 0 us
  starting transfers between devices: 11.3 us -> 0 us
  other arithmetic: 8.4 us -> 0 us
    all_gather x2 -> x0, blocking collectives: 70.5 us -> none  [the longest x1 44.4 us: local(): own_devices = lax.all_gather(flat_device, 'leaf', axis=0, tiled=True)]
    pallas_call x0 -> x1, Pallas kernels: none -> 28.4 us  [local(): pl.pallas_call(functools.partial(kernel, *sizes), out_shape=jax.ShapeDtyp...]
    dot_general x8 -> x0, matrix products: 15.3 us -> none  [the longest x1 5.29 us: local(): jnp.einsum('rtjq,tjpq->rtp', near_sources, near_blocks, preferred_element...]
    ppermute x4 -> x0, starting transfers between devices: 11.3 us -> none  [the longest x2 8.74 us: with_halo(): lax.ppermute(tail, axis, [(i, (i + 1) % count) for i in range(ends)])]
    gather x7 -> x0, local copies, waits for them, and re-layouts: 8.78 us -> none  [the longest x2 3.63 us: local(): jnp.take(coef_window, leaf_list - first_leaf + leaf_count, axis=0)]
    reshape x9 -> x0, local copies, waits for them, and re-layouts: 8.7 us -> none  [the longest x1 2.89 us: local(): leaf_coupling.reshape(rank_size, leaf_count, leaf_links, rank_size)]
    and x4 -> x0, other arithmetic: 2.27 us -> none  [the longest x1 0.6 us: local(): near_sources = jnp.take(near_rows, near_list - first_leaf + NR, axis=1)]
    all_gather x1 -> x0, other arithmetic: 2.22 us -> none  [local(): own_devices = lax.all_gather(flat_device, 'leaf', axis=0, tiled=True)]
  transfers between devices with their start and end apart: 4 -> 0, of which waited for: 0 -> 0; matrix products, arithmetic and copies ran while one was open for 23% -> 0% of each run, Pallas kernels for 0% -> 0%
where the time goes in v1:
time: 30.5 us; the launch traced here: 30.3 us
  Pallas kernels  28.4 us (93%)
  local copies, waits for them, and re-layouts  1.87 us (6%)
    pallas_call x1, Pallas kernels, local(): pl.pallas_call(functools.partial(kernel, *sizes), out_shape=jax.ShapeDtyp...  28.4 us
    unnamed x1, local copies, waits for them, and re-layouts  1.87 us

profile of v1, /device:TPU:1, one launch (start us, length us, event | category | flops | bytes accessed | tf_op | source)
XLA Modules:
  0.0 30.3 jit_solution(5823794556841341333)
XLA Ops:
  0.0 28.4 %shard_map.118 = bf16[64,4096]{1,0:T(8,128)(2,1)} custom-call(bf16[64,4096]{1,0:T(8,128)(2,1)} %panel.1, bf16[64,4096]{1,0:T(8,128)(2,1)} %basis.1, bf16[16,3,256,256]{3,2,1,0:T(8,128)(2,1)} %near.1, s32[3,16]{1,0:T(4,128)} %bitcast.3, bf16[64,1024]{1,0:T(8,128)(2,1)} %transfer_leaf.1, bf16[64,16384]{1,0:T(8,128)(2,1)} %transfer_device.1, ...), custom_call_target="tpu_custom_call" | custom-call | flops 500000000 | bytes 10000000 | tf_op jit(solution)/shard_map/pallas_call | solution.py:344
  28.4 1.9 %copy.14 = bf16[64,4096]{1,0:T(8,128)(2,1)} copy(bf16[64,4096]{1,0:T(8,128)(2,1)} %shard_map.118) | data formatting | bytes 1048576

commit v2 on v1

--- a/solution.py
+++ b/solution.py
@@ -46,6 +46,10 @@
     pieces = [x[:, i : i + 128] for i in range(0, x.shape[1], 128)]
     wide = [nn(piece, spreader()).astype(BF16) for piece in pieces]
     return jnp.concatenate(wide, axis=1)
+
+
+def farthest_first(count):
+    return sorted(range(1, count), key=lambda k: -min(k, count - k))
 
 
 def clamp(index, count):
@@ -75,9 +79,9 @@
     at_start, at_end = yi == 0, yi == ROW - 1
     next_z = jnp.where(at_start, lax.rem(zi + 1, cols), lax.rem(zi + cols - 1, cols)) * ROW + yi
 
-    row_peers = [zi * ROW + lax.rem(yi + k, ROW) for k in range(1, ROW)]
-    col_peers = [lax.rem(zi + k, cols) * ROW + yi for k in range(1, cols)]
-    grp_peers = [lax.rem(gi + k, groups) for k in range(1, groups)]
+    row_peers = [zi * ROW + lax.rem(yi + k, ROW) for k in farthest_first(ROW)]
+    col_peers = [lax.rem(zi + k, cols) * ROW + yi for k in farthest_first(cols)]
+    grp_peers = [lax.rem(gi + k, groups) for k in farthest_first(groups)]
 
     barrier = pltpu.get_barrier_semaphore()
     for peer in row_peers + col_peers:
@@ -97,11 +101,6 @@
     load_t = load(2, transfer_leaf, t_own)
     group_start = pl.multiple_of(gi * span * rank, span * rank)
     load_td = load(3, transfer_device.at[:, pl.ds(group_start, span * rank)], td_group)
-    load_self = load(4, near.at[:, 0], nb_self)
-    load_lc = load(5, leaf_coupling, lc)
-    load_gc = load(6, group_coupling, gc)
-    load_dc = load(7, device_coupling, dc)
-    load_rest = load(8, near.at[:, pl.ds(1, 2)], nb_rest)
 
     def send(src, dst, send_sem, recv_sem, device):
         copy = pltpu.make_async_remote_copy(
@@ -114,6 +113,11 @@
     low = low_lanes((64, 128))
     load_p.wait()
     load_b.wait()
+    load_gc = load(6, group_coupling, gc)
+    load_dc = load(7, device_coupling, dc)
+    load_self = load(4, near.at[:, 0], nb_self)
+    load_lc = load(5, leaf_coupling, lc)
+    load_rest = load(8, near.at[:, pl.ds(1, 2)], nb_rest)
     for pair in range(leaves // 2):
         wide = []
         for leaf in (2 * pair, 2 * pair + 1):
@@ -139,9 +143,18 @@
     to_right, to_left = jnp.where(at_end, 2, 0), jnp.where(at_start, 2, 1)
     edges = {
         "c": (halo_c, 0, c_own, c_own),
-        "a": (halo_a, 3, p_own.at[pl.ds(leaves - half, half)], p_own.at[pl.ds(0, half)]),
-        "b": (halo_b, 6, p_own.at[pl.ds(leaves - 2 * half, half)], p_own.at[pl.ds(half, half)]),
     }
+    piece = half // 2
+    for n, (name, buffer, from_end, from_start) in enumerate(
+        (("a", halo_a, leaves - half, 0), ("b", halo_b, leaves - 2 * half, half))
+    ):
+        for k in (0, 1):
+            edges[name + str(k)] = (
+                buffer.at[:, pl.ds(k * piece, piece)],
+                3 + 6 * n + 3 * k,
+                p_own.at[pl.ds(from_end + k * piece, piece)],
+                p_own.at[pl.ds(from_start + k * piece, piece)],
+            )
     halo_copies = []
 
     def halo_copy(name, src, slot, k, device):
@@ -151,30 +164,32 @@
             recv_sem=halo_recv.at[base + slot], device_id=(gi, device), device_id_type=MESH,
         )
 
+    has_left, has_right = li > 0, li < span - 1
+    hands_on = (at_start & (zi < cols - 1)) | (at_end & (zi > 0))
+
     def send_halo(name):
-        for k, (slot, device) in enumerate(((to_right, right), (to_left, left))):
+        for k, (slot, device, needed) in enumerate(((to_right, right, has_right), (to_left, left, has_left))):
             copy = halo_copy(name, edges[name][2 + k], slot, k, device)
-            copy.start()
-            halo_copies.append(copy)
+            pl.when(needed)(copy.start)
+            halo_copies.append((needed, copy))
 
     def hand_on(name):
-        @pl.when(at_start | at_end)
+        @pl.when(hands_on)
         def _():
             buffer = edges[name][0]
             halo_copy(name, buffer.at[2], 2, 2, next_z).wait_recv()
             halo_copy(name, buffer.at[2], jnp.where(at_start, 0, 1), 2, next_z).start()
 
     def wait_halo(name):
-        for slot in (0, 1):
-            halo_copy(name, edges[name][0].at[2], slot, 2, next_z).wait_recv()
+        for slot, needed in ((0, has_left), (1, has_right)):
+            pl.when(needed)(halo_copy(name, edges[name][0].at[2], slot, 2, next_z).wait_recv)
 
     def end_halo(name):
-        @pl.when(at_start | at_end)
-        def _():
-            halo_copy(name, edges[name][0].at[2], 0, 2, next_z).wait_send()
+        pl.when(hands_on)(halo_copy(name, edges[name][0].at[2], 0, 2, next_z).wait_send)
 
     send_halo("c")
-    send_halo("a")
+    send_halo("a0")
+    send_halo("a1")
 
     load_td.wait()
     for j in range(cols):
@@ -199,25 +214,26 @@
     td_wide = jnp.concatenate([td_wide, td_wide], axis=0)
 
     for copy in col_copies:
-        copy.wait()
+        copy.wait_recv()
     col_d = jnp.concatenate([dbuf[yi * cols + j] for j in range(cols)], axis=1)
     pgbuf[yi] = fold_rows(nt(unfold_rows(col_d), td_wide))
     pg_copies = [
         send(pgbuf.at[yi], pgbuf.at[yi], row_send.at[k], row_recv.at[k], (gi, peer))
         for k, peer in enumerate(row_peers)
     ]
-    send_halo("b")
+    send_halo("b0")
+    send_halo("b1")
     mine = pl.ds(yi * cols, cols)
     d_copies = [
         send(dbuf.at[mine], dbuf.at[mine], drow_send.at[k], drow_recv.at[k], (gi, peer))
         for k, peer in enumerate(row_peers)
     ]
 
-    hand_on("c")
-    hand_on("a")
+    for name in ("c", "a0", "a1"):
+        hand_on(name)
 
     for copy in pg_copies:
-        copy.wait()
+        copy.wait_recv()
     total = pgbuf[0]
     for j in range(1, ROW):
         total = total + pgbuf[j]
@@ -227,7 +243,8 @@
         for k, peer in enumerate(grp_peers)
     ]
 
-    hand_on("b")
+    for name in ("b0", "b1"):
+        hand_on(name)
 
     load_lc.wait()
     wait_halo("c")
@@ -270,17 +287,28 @@
         return nt(jnp.concatenate(found, axis=1), jnp.concatenate(blocks, axis=1))
 
     load_rest.wait()
-    wait_halo("a")
+    wait_halo("a0")
+    wait_halo("a1")
     for leaf in range(half, leaves - half):
         acc[:, leaf * ls : (leaf + 1) * ls] += near_rest(leaf)
 
+    outer = list(range(half)) + list(range(leaves - half, leaves))
+    handed_on = (at_start & has_left) | (at_end & has_right)
+
+    @pl.when(jnp.logical_not(handed_on))
+    def _():
+        wait_halo("b0")
+        wait_halo("b1")
+        for leaf in outer:
+            acc[:, leaf * ls : (leaf + 1) * ls] += near_rest(leaf)
+
     for copy in d_copies:
-        copy.wait()
+        copy.wait_recv()
     places = [clamp(device_list[0, j] - gi * span, span) for j in range(device_links)]
     found = [dbuf[place % ROW * cols + place // ROW] for place in places]
     d_far = nt(unfold_rows(jnp.concatenate(found, axis=1)), dc_dup)
     for copy in g_copies:
-        copy.wait()
+        copy.wait_recv()
     found = [gbuf[clamp(group_list[0, j], groups)] for j in range(group_links)]
     g_local = nt(unfold_rows(jnp.concatenate(found, axis=1)), gc_dup).astype(BF16)
     td_own = td_of(zi)[:, :rank]
@@ -294,18 +322,23 @@
         second = slice((2 * pair + 1) * ls, (2 * pair + 2) * ls)
         far = nn(stacked, jnp.concatenate([b_own[:, first], b_own[:, second]], axis=0))
         for leaf, lanes, part in ((2 * pair, first, far[:64]), (2 * pair + 1, second, far[64:])):
-            if half <= leaf < leaves - half:
-                out[:, lanes] = (acc[:, lanes] + part).astype(BF16)
-            else:
-                acc[:, lanes] = acc[:, lanes] + part
-
-    wait_halo("b")
-    for leaf in list(range(half)) + list(range(leaves - half, leaves)):
-        lanes = slice(leaf * ls, (leaf + 1) * ls)
-        out[:, lanes] = (acc[:, lanes] + near_rest(leaf)).astype(BF16)
-
-    for copy in halo_copies:
+            sums = acc[:, lanes] + part
+            out[:, lanes] = sums.astype(BF16)
+            if leaf in outer:
+                acc[:, lanes] = sums
+
+    @pl.when(handed_on)
+    def _():
+        wait_halo("b0")
+        wait_halo("b1")
+        for leaf in outer:
+            lanes = slice(leaf * ls, (leaf + 1) * ls)
+            out[:, lanes] = (acc[:, lanes] + near_rest(leaf)).astype(BF16)
+
+    for copy in col_copies + pg_copies + d_copies + g_copies:
         copy.wait_send()
+    for needed, copy in halo_copies:
+        pl.when(needed)(copy.wait_send)
     for name in edges:
         end_halo(name)
 
@@ -343,7 +376,7 @@
     halo = pltpu.VMEM((3, half, rhs, ls), BF16)
     return pl.pallas_call(
         functools.partial(kernel, *sizes),
-        out_shape=jax.ShapeDtypeStruct((rhs, width), BF16),
+        out_shape=pltpu.VMEM((rhs, width), BF16),
         in_specs=[hbm, hbm, hbm, smem, hbm, hbm, hbm, smem, hbm, smem, hbm, smem],
         out_specs=pl.BlockSpec(memory_space=pltpu.VMEM),
         scratch_shapes=[
@@ -368,8 +401,8 @@
             pltpu.VMEM((rhs, coefs), F32),
             pltpu.VMEM((rank, cols * 4 * rank), BF16),
             dma((9,)),
-            dma((9,)),
-            dma((9,)),
+            dma((15,)),
+            dma((15,)),
             dma((ROW - 1,)),
             dma((ROW - 1,)),
             dma((cols - 1,)),

time: 30.5 us -> 27.2 us (0.89)
  Pallas kernels: 28.4 us -> 26.1 us
  local copies, waits for them, and re-layouts: 1.87 us -> 0.8 us
    pallas_call x1, Pallas kernels: 28.4 us -> 26.1 us  [local(): pl.pallas_call(functools.partial(kernel, *sizes), out_shape=pltpu.VMEM((r...]
    unnamed x1, local copies, waits for them, and re-layouts: 1.87 us -> 0.8 us
where the time goes in v2:
time: 27.2 us; the launch traced here: 26.9 us
  Pallas kernels  26.1 us (96%)
  local copies, waits for them, and re-layouts  0.8 us (3%)
    pallas_call x1, Pallas kernels, local(): pl.pallas_call(functools.partial(kernel, *sizes), out_shape=pltpu.VMEM((r...  26.1 us
    unnamed x1, local copies, waits for them, and re-layouts  0.8 us

profile of v2, /device:TPU:1, one launch (start us, length us, event | category | flops | bytes accessed | tf_op | source)
XLA Modules:
  0.0 26.9 jit_solution(8566775483142843169)
XLA Ops:
  0.0 26.1 %shard_map.118 = bf16[64,4096]{1,0:T(8,128)(2,1)S(1)} custom-call(bf16[64,4096]{1,0:T(8,128)(2,1)} %panel.1, bf16[64,4096]{1,0:T(8,128)(2,1)} %basis.1, bf16[16,3,256,256]{3,2,1,0:T(8,128)(2,1)} %near.1, s32[3,16]{1,0:T(4,128)} %bitcast.3, bf16[64,1024]{1,0:T(8,128)(2,1)} %transfer_leaf.1, bf16[64,16384]{1,0:T(8,128)(2,1)} %transfer_device.1, ...), custom_call_target="tpu_custom_call" | custom-call | flops 500000000 | bytes 10000000 | tf_op jit(solution)/shard_map/pallas_call | solution.py:377
  26.1 0.8 %copy.14 = bf16[64,4096]{1,0:T(8,128)(2,1)} copy(bf16[64,4096]{1,0:T(8,128)(2,1)S(1)} %shard_map.118) | data formatting | bytes 1048576

commit v3 on v2

--- a/solution.py
+++ b/solution.py
@@ -58,12 +58,13 @@
 
 def kernel(
     groups, span, leaves, rank, ls, leaf_links, device_links, group_links, reach,
-    panel, basis, near, near_list, transfer_leaf, transfer_device, leaf_coupling, leaf_list,
-    device_coupling, device_list, group_coupling, group_list,
+    panel, basis, near, near_hbm, transfer_leaf, transfer_device, leaf_coupling, leaf_hbm,
+    device_coupling, device_hbm, group_coupling, group_hbm,
     out,
     p_own, b_own, nb_self, nb_rest, t_own, td_group, lc, dc, gc,
     halo_a, halo_b, c_own, halo_c, dbuf, pgbuf, gbuf,
     w, acc, lf, td_dup,
+    near_list, leaf_list, device_list, group_list,
     load_sem, halo_send, halo_recv, row_send, row_recv, col_send, col_recv, drow_send, drow_recv,
     grp_send, grp_recv,
 ):
@@ -84,10 +85,13 @@
     grp_peers = [lax.rem(gi + k, groups) for k in farthest_first(groups)]
 
     barrier = pltpu.get_barrier_semaphore()
-    for peer in row_peers + col_peers:
+    next_left, next_right = lax.rem(li + span - 1, span), lax.rem(li + 1, span)
+    for peer in col_peers:
         pl.semaphore_signal(barrier, inc=1, device_id=(gi, peer), device_id_type=MESH)
     for peer in grp_peers:
         pl.semaphore_signal(barrier, inc=1, device_id=(peer, li), device_id_type=MESH)
+    for peer in row_peers + [next_left, next_right]:
+        pl.semaphore_signal(barrier, inc=1, device_id=(gi, peer), device_id_type=MESH)
 
     def load(i, src, dst):
         copy = pltpu.make_async_copy(src, dst, load_sem.at[i])
@@ -113,6 +117,12 @@
     low = low_lanes((64, 128))
     load_p.wait()
     load_b.wait()
+    load_lists = [
+        load(9 + i, src, dst)
+        for i, (src, dst) in enumerate(
+            ((near_hbm, near_list), (leaf_hbm, leaf_list), (device_hbm, device_list), (group_hbm, group_list))
+        )
+    ]
     load_gc = load(6, group_coupling, gc)
     load_dc = load(7, device_coupling, dc)
     load_self = load(4, near.at[:, 0], nb_self)
@@ -134,7 +144,7 @@
     own_slot = yi * cols + zi
     dbuf[own_slot] = fold_rows(own_d).astype(BF16)
 
-    pl.semaphore_wait(barrier, (ROW - 1) + (cols - 1) + (groups - 1))
+    pl.semaphore_wait(barrier, 2 + (ROW - 1) + (cols - 1) + (groups - 1))
 
     col_copies = [
         send(dbuf.at[own_slot], dbuf.at[own_slot], col_send.at[k], col_recv.at[k], (gi, peer))
@@ -168,7 +178,10 @@
     hands_on = (at_start & (zi < cols - 1)) | (at_end & (zi > 0))
 
     def send_halo(name):
-        for k, (slot, device, needed) in enumerate(((to_right, right, has_right), (to_left, left, has_left))):
+        targets = ((to_right, right, has_right), (to_left, left, has_left))
+        if name == "c":
+            targets = ((0, next_right, has_right), (1, next_left, has_left))
+        for k, (slot, device, needed) in enumerate(targets):
             copy = halo_copy(name, edges[name][2 + k], slot, k, device)
             pl.when(needed)(copy.start)
             halo_copies.append((needed, copy))
@@ -182,7 +195,7 @@
 
     def wait_halo(name):
         for slot, needed in ((0, has_left), (1, has_right)):
-            pl.when(needed)(halo_copy(name, edges[name][0].at[2], slot, 2, next_z).wait_recv)
+            pl.when(needed)(halo_copy(name, edges[name][0].at[slot], slot, 2, next_z).wait_recv)
 
     def end_halo(name):
         pl.when(hands_on)(halo_copy(name, edges[name][0].at[2], 0, 2, next_z).wait_send)
@@ -229,7 +242,7 @@
         for k, peer in enumerate(row_peers)
     ]
 
-    for name in ("c", "a0", "a1"):
+    for name in ("a0", "a1"):
         hand_on(name)
 
     for copy in pg_copies:
@@ -246,6 +259,8 @@
     for name in ("b0", "b1"):
         hand_on(name)
 
+    for copy in load_lists:
+        copy.wait()
     load_lc.wait()
     wait_halo("c")
     for slot, start in ((0, 0), (1, 2 * leaves)):
@@ -339,7 +354,7 @@
         copy.wait_send()
     for needed, copy in halo_copies:
         pl.when(needed)(copy.wait_send)
-    for name in edges:
+    for name in ("a0", "a1", "b0", "b1"):
         end_halo(name)
 
 
@@ -370,14 +385,13 @@
     group_links = group_list.shape[1]
     coefs = leaves * rank
     hbm = pl.BlockSpec(memory_space=pltpu.HBM)
-    smem = pl.BlockSpec(memory_space=pltpu.SMEM)
     sizes = (groups, span, leaves, rank, ls, leaf_links, device_links, group_links, reach)
     dma = pltpu.SemaphoreType.DMA
     halo = pltpu.VMEM((3, half, rhs, ls), BF16)
     return pl.pallas_call(
         functools.partial(kernel, *sizes),
         out_shape=pltpu.VMEM((rhs, width), BF16),
-        in_specs=[hbm, hbm, hbm, smem, hbm, hbm, hbm, smem, hbm, smem, hbm, smem],
+        in_specs=[hbm] * 12,
         out_specs=pl.BlockSpec(memory_space=pltpu.VMEM),
         scratch_shapes=[
             pltpu.VMEM((leaves, rhs, ls), BF16),
@@ -392,7 +406,7 @@
             halo,
             halo,
             pltpu.VMEM((rhs, coefs), BF16),
-            pltpu.VMEM((3, rhs, coefs), BF16),
+            pltpu.VMEM((2, rhs, coefs), BF16),
             pltpu.VMEM((span, rhs // 2, 2 * rank), BF16),
             pltpu.VMEM((ROW, rhs // 2, 2 * rank), F32),
             pltpu.VMEM((groups, rhs // 2, 2 * rank), BF16),
@@ -400,7 +414,11 @@
             pltpu.VMEM((rhs, width), F32),
             pltpu.VMEM((rhs, coefs), F32),
             pltpu.VMEM((rank, cols * 4 * rank), BF16),
-            dma((9,)),
+            pltpu.SMEM((near_links, leaves), jnp.int32),
+            pltpu.SMEM((leaf_links, leaves), jnp.int32),
+            pltpu.SMEM((1, device_links), jnp.int32),
+            pltpu.SMEM((1, group_links), jnp.int32),
+            dma((13,)),
             dma((15,)),
             dma((15,)),
             dma((ROW - 1,)),

time: 27.2 us -> 26 us (0.956)
  Pallas kernels: 26.1 us -> 25.1 us
    pallas_call x1, Pallas kernels: 26.1 us -> 25.1 us  [local(): pl.pallas_call(functools.partial(kernel, *sizes), out_shape=pltpu.VMEM((r...]
where the time goes in v3:
time: 26 us; the launch traced here: 25.9 us
  Pallas kernels  25.1 us (97%)
  local copies, waits for them, and re-layouts  0.8 us (3%)
    pallas_call x1, Pallas kernels, local(): pl.pallas_call(functools.partial(kernel, *sizes), out_shape=pltpu.VMEM((r...  25.1 us
    unnamed x1, local copies, waits for them, and re-layouts  0.8 us

profile of v3, /device:TPU:1, one launch (start us, length us, event | category | flops | bytes accessed | tf_op | source)
XLA Modules:
  0.0 25.9 jit_solution(617210127028503503)
XLA Ops:
  0.0 25.1 %shard_map.118 = bf16[64,4096]{1,0:T(8,128)(2,1)S(1)} custom-call(bf16[64,4096]{1,0:T(8,128)(2,1)} %panel.1, bf16[64,4096]{1,0:T(8,128)(2,1)} %basis.1, bf16[16,3,256,256]{3,2,1,0:T(8,128)(2,1)} %near.1, s32[3,16]{1,0:T(4,128)} %bitcast.3, bf16[64,1024]{1,0:T(8,128)(2,1)} %transfer_leaf.1, bf16[64,16384]{1,0:T(8,128)(2,1)} %transfer_device.1, ...), custom_call_target="tpu_custom_call" | custom-call | flops 500000000 | bytes 10000000 | tf_op jit(solution)/shard_map/pallas_call | solution.py:391
  25.1 0.8 %copy.14 = bf16[64,4096]{1,0:T(8,128)(2,1)} copy(bf16[64,4096]{1,0:T(8,128)(2,1)S(1)} %shard_map.118) | data formatting | bytes 1048576

commit v4 on v3

--- a/solution.py
+++ b/solution.py
@@ -127,7 +127,6 @@
     load_dc = load(7, device_coupling, dc)
     load_self = load(4, near.at[:, 0], nb_self)
     load_lc = load(5, leaf_coupling, lc)
-    load_rest = load(8, near.at[:, pl.ds(1, 2)], nb_rest)
     for pair in range(leaves // 2):
         wide = []
         for leaf in (2 * pair, 2 * pair + 1):
@@ -226,10 +225,12 @@
     td_wide = jnp.concatenate([td_of(j) for j in range(cols)], axis=1)
     td_wide = jnp.concatenate([td_wide, td_wide], axis=0)
 
+    load_rest = load(8, near.at[:, pl.ds(1, 2)], nb_rest)
+
     for copy in col_copies:
         copy.wait_recv()
     col_d = jnp.concatenate([dbuf[yi * cols + j] for j in range(cols)], axis=1)
-    pgbuf[yi] = fold_rows(nt(unfold_rows(col_d), td_wide))
+    pgbuf[yi] = fold_rows(nt(unfold_rows(col_d), td_wide)).astype(BF16)
     pg_copies = [
         send(pgbuf.at[yi], pgbuf.at[yi], row_send.at[k], row_recv.at[k], (gi, peer))
         for k, peer in enumerate(row_peers)
@@ -247,9 +248,9 @@
 
     for copy in pg_copies:
         copy.wait_recv()
-    total = pgbuf[0]
+    total = pgbuf[0].astype(F32)
     for j in range(1, ROW):
-        total = total + pgbuf[j]
+        total = total + pgbuf[j].astype(F32)
     gbuf[gi] = total.astype(BF16)
     g_copies = [
         send(gbuf.at[gi], gbuf.at[gi], grp_send.at[k], grp_recv.at[k], (peer, li))
@@ -408,7 +409,7 @@
             pltpu.VMEM((rhs, coefs), BF16),
             pltpu.VMEM((2, rhs, coefs), BF16),
             pltpu.VMEM((span, rhs // 2, 2 * rank), BF16),
-            pltpu.VMEM((ROW, rhs // 2, 2 * rank), F32),
+            pltpu.VMEM((ROW, rhs // 2, 2 * rank), BF16),
             pltpu.VMEM((groups, rhs // 2, 2 * rank), BF16),
             pltpu.VMEM((3 * leaves, rhs, 2 * rank), BF16),
             pltpu.VMEM((rhs, width), F32),

time: 26 us -> 25.9 us (level)
  no operation moved by 1% of the time
where the time goes in v4:
time: 25.9 us; the launch traced here: 25.8 us
  Pallas kernels  25 us (97%)
  local copies, waits for them, and re-layouts  0.8 us (3%)
    pallas_call x1, Pallas kernels, local(): pl.pallas_call(functools.partial(kernel, *sizes), out_shape=pltpu.VMEM((r...  25 us
    unnamed x1, local copies, waits for them, and re-layouts  0.8 us

profile of v4, /device:TPU:1, one launch (start us, length us, event | category | flops | bytes accessed | tf_op | source)
XLA Modules:
  0.0 25.8 jit_solution(4715108169498818942)
XLA Ops:
  0.0 25.0 %shard_map.118 = bf16[64,4096]{1,0:T(8,128)(2,1)S(1)} custom-call(bf16[64,4096]{1,0:T(8,128)(2,1)} %panel.1, bf16[64,4096]{1,0:T(8,128)(2,1)} %basis.1, bf16[16,3,256,256]{3,2,1,0:T(8,128)(2,1)} %near.1, s32[3,16]{1,0:T(4,128)} %bitcast.3, bf16[64,1024]{1,0:T(8,128)(2,1)} %transfer_leaf.1, bf16[64,16384]{1,0:T(8,128)(2,1)} %transfer_device.1, ...), custom_call_target="tpu_custom_call" | custom-call | flops 500000000 | bytes 10000000 | tf_op jit(solution)/shard_map/pallas_call | solution.py:392
  25.0 0.8 %copy.14 = bf16[64,4096]{1,0:T(8,128)(2,1)} copy(bf16[64,4096]{1,0:T(8,128)(2,1)S(1)} %shard_map.118) | data formatting | bytes 1048576
